TPU v7x, 512 devices: a whole 4x4x16 slice. The times are simulated.
512 devices in a mesh: sx: 32 (over y, x, core), sy: 16 (over z).
Axes of the slice: x: 4, y: 4, z: 16, core: 2. Of those that a mesh axis runs over, the one named last changes fastest.
Arguments:
- inputs: bfloat16 [65536, 4096], P(('sx', 'sy')), may hold values from -6 to 6
- keys_in: bfloat16 [65536, 128], P(('sx', 'sy')), may hold values from -6 to 6
- queries: bfloat16 [65536, 128], P(('sx', 'sy')), may hold values from -6 to 6
- step_sizes: float32 [65536, 64], P(('sx', 'sy')), may hold values from 0.01 to 0.1
- level_weights: float32 [20, 64], replicated, may hold values from 0.3 to 3
- skip_gain: float32 [64], replicated, may hold values from 0.5 to 1.5
Outputs:
- outputs: bfloat16 [65536, 4096], P(('sx', 'sy'))
All inputs are finite; a program needn't handle non-finite values.
Results may differ from a plain program's by a relative error of at most 0.005.
Values sent between devices are 32-bit elements; how exact they have to be, the bound alone decides.
A program may use at most 64 MiB of HBM per device.

v0:
```python
import jax
import jax.numpy as jnp
from jax import lax
from jax.sharding import PartitionSpec as P

STRETCH = 64


def swapped(block, axis, distance):
    count = lax.axis_size(axis)
    route = []
    for low in range(count):
        high = low | 1 << distance
        if high != low and high < count:
            route += [(low, high), (high, low)]
    return lax.ppermute(block, axis, route)


def add_level(outputs, folded, queries_f32, partner, scale_vec):
    term = partner * scale_vec[None, :]
    return (outputs + jnp.dot(queries_f32, term, precision=lax.Precision.HIGHEST), folded)


def high_levels(
    my_columns, level_weights, index_low, index_high, head_share, head_dim, first_depth, bits_high
):
    high_sum = jnp.zeros_like(my_columns)
    for level_bit in range(bits_high):
        partner = swapped(my_columns, "sx", level_bit)
        upper_half = (index_high // 2**level_bit % 2).astype(jnp.float32)
        level_depth = first_depth + level_bit
        row_share = lax.dynamic_slice_in_dim(
            level_weights[level_depth + 1], index_low * head_share, head_share, 0
        )
        scale_vec = upper_half * jnp.repeat(
            row_share * (2.0**level_depth * STRETCH) ** (-0.5), head_dim
        )
        high_sum = high_sum + partner * scale_vec[None, :]
        my_columns = my_columns + partner
    return high_sum


def on_device(inputs, keys_in, queries, step_sizes, level_weights, skip_gain):
    tok_rows, full_width = inputs.shape
    num_heads = step_sizes.shape[1]
    head_dim = full_width // num_heads
    state_dim = keys_in.shape[1]
    block_count = tok_rows // STRETCH
    local_bits = block_count.bit_length() - 1
    highest = lax.Precision.HIGHEST
    values = (
        (inputs.astype(jnp.float32).reshape(tok_rows, num_heads, head_dim) * step_sizes[:, :, None])
        .reshape(tok_rows, full_width)
        .astype(jnp.bfloat16)
    )
    key_blocks = keys_in.reshape(block_count, STRETCH, state_dim)
    query_blocks = queries.reshape(block_count, STRETCH, state_dim)
    value_blocks = values.reshape(block_count, STRETCH, full_width)
    block_states = jnp.einsum(
        "bcn,bcw->bnw", key_blocks, value_blocks, preferred_element_type=jnp.float32
    )
    scores = jnp.einsum(
        "btn,bsn->bts", query_blocks, key_blocks, preferred_element_type=jnp.float32
    )
    causal = lax.broadcasted_iota(jnp.int32, (STRETCH, STRETCH), 0) >= lax.broadcasted_iota(
        jnp.int32, (STRETCH, STRETCH), 1
    )
    scores = jnp.where(causal[None], scores, 0.0) * STRETCH ** (-0.5)
    intra_weights = (scores[:, None] * level_weights[0][None, :, None, None]).astype(jnp.bfloat16)
    intra_out = jnp.einsum(
        "bhts,bshp->bthp",
        intra_weights,
        value_blocks.reshape(block_count, STRETCH, num_heads, head_dim),
        preferred_element_type=jnp.float32,
    ).reshape(tok_rows, full_width)
    outputs = inputs.astype(jnp.float32) * jnp.repeat(skip_gain, head_dim)[None, :] + intra_out
    queries_f32 = queries.astype(jnp.float32)
    level_bit = 0
    half_span = 2**level_bit
    groups = block_count // (2 * half_span)
    lower_sum = block_states.reshape(groups, 2, half_span, state_dim, full_width)[:, 0].sum(axis=1)
    scale_vec = jnp.repeat(level_weights[level_bit + 1] * (half_span * STRETCH) ** (-0.5), head_dim)
    upper_rows = queries_f32.reshape(groups, 2, half_span * STRETCH, state_dim)[:, 1]
    level_part = jnp.einsum(
        "gtn,gnw->gtw", upper_rows, lower_sum * scale_vec[None, None, :], precision=highest
    )
    outputs = outputs + jnp.stack([jnp.zeros_like(level_part), level_part], axis=1).reshape(
        tok_rows, full_width
    )
    size_low = lax.axis_size("sy")
    size_high = lax.axis_size("sx")
    bits_low = size_low.bit_length() - 1
    bits_high = size_high.bit_length() - 1
    index_low = lax.axis_index("sy")
    index_high = lax.axis_index("sx")
    head_share = num_heads // size_low
    share_width = head_share * head_dim
    group_sum = block_states.sum(axis=0)
    folded = jnp.zeros((state_dim, full_width), jnp.float32)
    for level_bit in range(bits_low):
        partner = swapped(group_sum, "sy", level_bit)
        upper_half = (index_low // 2**level_bit % 2).astype(jnp.float32)
        level_depth = local_bits + level_bit
        scale_vec = upper_half * jnp.repeat(
            level_weights[level_depth + 1] * (2.0**level_depth * STRETCH) ** (-0.5), head_dim
        )
        outputs, folded = add_level(outputs, folded, queries_f32, partner, scale_vec)
        group_sum = group_sum + partner
    my_columns = lax.dynamic_slice_in_dim(group_sum, index_low * share_width, share_width, 1)
    high_sum = high_levels(
        my_columns,
        level_weights,
        index_low,
        index_high,
        head_share,
        head_dim,
        local_bits + bits_low,
        bits_high,
    )
    outputs = outputs + jnp.dot(
        queries_f32,
        lax.all_gather(high_sum, "sy", axis=1, tiled=True),
        precision=lax.Precision.HIGHEST,
    )
    return outputs.astype(jnp.bfloat16)


def solution(mesh):
    placed = (
        P(("sx", "sy"), None),
        P(("sx", "sy"), None),
        P(("sx", "sy"), None),
        P(("sx", "sy"), None),
        P(),
        P(),
    )
    return jax.shard_map(
        on_device, mesh=mesh, in_specs=placed, out_specs=P(("sx", "sy"), None), check_vma=False
    )
```

profile of v0, /device:TPU:4, one launch (start us, length us, event | category | flops | bytes accessed | tf_op | source)
XLA Modules:
  0.0 711.0 jit_solution(6802354924683908111)
XLA Ops:
  9.0 3.0 bitcast_reduce_fusion
  12.0 3.8 collective-permute-start
  15.8 45.6 %collective-permute-done = f32[128,4096]{0,1:T(8,128)S(1)} collective-permute-done((f32[128,4096]{0,1:T(8,128)S(1)}, f32[128,4096]{0,1:T(8,128)S(1)}, u32[]{:S(2)}, u32[]{:S(2)}) %collective-permute-start) | collective-permute-done | bytes 2097184 | tf_op jit(solution)/shard_map/ppermute | solution.py:16
  63.0 5.2 collective-permute-start.1
  68.2 89.9 %collective-permute-done.1 = f32[128,4096]{0,1:T(8,128)S(1)} collective-permute-done((f32[128,4096]{0,1:T(8,128)S(1)}, f32[128,4096]{0,1:T(8,128)S(1)}, u32[]{:S(2)}, u32[]{:S(2)}) %collective-permute-start.1) | collective-permute-done | bytes 2097184 | tf_op jit(solution)/shard_map/ppermute | solution.py:16
  159.5 9.1 %collective-permute-start.2 = (f32[128,4096]{0,1:T(8,128)S(1)}, f32[128,4096]{0,1:T(8,128)S(1)}, u32[]{:S(2)}, u32[]{:S(2)}) collective-permute-start(f32[128,4096]{0,1:T(8,128)S(1)} %add.113), channel_id=1, source_target_pairs={{0,4},{4,0},{1,5},{5,1},{2,6},{6,2},{3,7},{7,3},{8,12},{12,8},{9,1... | collective-permute-start | bytes 6291464 | tf_op jit(solution)/shard_map/ppermute | solution.py:16
  168.6 223.9 %collective-permute-done.2 = f32[128,4096]{0,1:T(8,128)S(1)} collective-permute-done((f32[128,4096]{0,1:T(8,128)S(1)}, f32[128,4096]{0,1:T(8,128)S(1)}, u32[]{:S(2)}, u32[]{:S(2)}) %collective-permute-start.2) | collective-permute-done | bytes 2097184 | tf_op jit(solution)/shard_map/ppermute | solution.py:16
  394.4 103.3 %collective-permute-start.3 = (f32[128,4096]{0,1:T(8,128)}, f32[128,4096]{0,1:T(8,128)}, u32[]{:S(2)}, u32[]{:S(2)}) collective-permute-start(f32[128,4096]{0,1:T(8,128)} %add.116), channel_id=1, source_target_pairs={{0,8},{8,0},{1,9},{9,1},{2,10},{10,2},{3,11},{11,3},{4,12},{12,4},... | collective-permute-start | bytes 6291464 | tf_op jit(solution)/shard_map/ppermute | solution.py:16
  497.7 91.3 %collective-permute-done.3 = f32[128,4096]{0,1:T(8,128)} collective-permute-done((f32[128,4096]{0,1:T(8,128)}, f32[128,4096]{0,1:T(8,128)}, u32[]{:S(2)}, u32[]{:S(2)}) %collective-permute-start.3) | collective-permute-done | bytes 2097184 | tf_op jit(solution)/shard_map/ppermute | solution.py:16
  593.2 3.1 collective-permute-start.5
  596.3 4.3 collective-permute-done.5
  603.2 5.9 collective-permute-done.6
  609.1 3.5 collective-permute-start.7
  615.9 5.3 collective-permute-start.8
  628.1 2.9 convolution_bitcast_fusion.6
  631.0 5.8 copy.26
  636.8 5.4 reshape.209
  642.2 3.0 convolution_bitcast_fusion.5
  646.7 3.0 copy.24
  649.8 2.5 convolution_bitcast_fusion.3
  654.7 4.2 convolution_bitcast_fusion.1
  658.9 34.8 %all-gather.2.cloned.1.call-done = f32[128,4096]{0,1:T(8,128)} async-done(((f32[128,256]{0,1:T(8,128)}), f32[128,4096]{0,1:T(8,128)}) %all-gather.2.cloned.1.call-update) | async-done | bytes 2097168 | tf_op jit(solution)/shard_map/all_gather | solution.py:122
  693.7 2.8 convolution_bitcast_fusion
  696.5 5.3 fusion.5
  (73 shorter events, 30.3 us)
Async XLA Ops:
  6.5 2.4 copy-start
  6.5 1.6 copy-start.9
  6.5 687.2 %all-gather.2.cloned.1.call-start = ((), (), s32[]{:S(2)}) async-start(), calls=%async_computation | async-start | bytes 2228224 | tf_op jit(solution)/shard_map/all_gather | solution.py:122
  12.0 49.4 %collective-permute-start = (f32[128,4096]{0,1:T(8,128)S(1)}, f32[128,4096]{0,1:T(8,128)S(1)}, u32[]{:S(2)}, u32[]{:S(2)}) collective-permute-start(f32[128,4096]{0,1:T(8,128)S(1)} %get-tuple-element.16), channel_id=1, source_target_pairs={{0,1},{1,0},{2,3},{3,2},{4,5},{5,4},{6,7},{7,6},{8,9},{9,8},{10,11... | collective-permute-start | bytes 6291464 | tf_op jit(solution)/shard_map/ppermute | solution.py:16
  61.4 1.4 copy-start.5
  63.0 95.1 %collective-permute-start.1 = (f32[128,4096]{0,1:T(8,128)S(1)}, f32[128,4096]{0,1:T(8,128)S(1)}, u32[]{:S(2)}, u32[]{:S(2)}) collective-permute-start(f32[128,4096]{0,1:T(8,128)S(1)} %add.110), channel_id=1, source_target_pairs={{0,2},{2,0},{1,3},{3,1},{4,6},{6,4},{5,7},{7,5},{8,10},{10,8},{9,1... | collective-permute-start | bytes 6291464 | tf_op jit(solution)/shard_map/ppermute | solution.py:16
  158.1 1.3 copy-start.1
  159.5 233.0 %collective-permute-start.2 = (f32[128,4096]{0,1:T(8,128)S(1)}, f32[128,4096]{0,1:T(8,128)S(1)}, u32[]{:S(2)}, u32[]{:S(2)}) collective-permute-start(f32[128,4096]{0,1:T(8,128)S(1)} %add.113), channel_id=1, source_target_pairs={{0,4},{4,0},{1,5},{5,1},{2,6},{6,2},{3,7},{7,3},{8,12},{12,8},{9,1... | collective-permute-start | bytes 6291464 | tf_op jit(solution)/shard_map/ppermute | solution.py:16
  392.4 2.0 copy-start.3
  394.4 194.6 %collective-permute-start.3 = (f32[128,4096]{0,1:T(8,128)}, f32[128,4096]{0,1:T(8,128)}, u32[]{:S(2)}, u32[]{:S(2)}) collective-permute-start(f32[128,4096]{0,1:T(8,128)} %add.116), channel_id=1, source_target_pairs={{0,8},{8,0},{1,9},{9,1},{2,10},{10,2},{3,11},{11,3},{4,12},{12,4},... | collective-permute-start | bytes 6291464 | tf_op jit(solution)/shard_map/ppermute | solution.py:16
  589.9 3.2 collective-permute-start.4
  593.2 7.4 %collective-permute-start.5 = (f32[128,256]{0,1:T(8,128)S(1)}, f32[128,256]{0,1:T(8,128)S(1)}, u32[]{:S(2)}, u32[]{:S(2)}) collective-permute-start(f32[128,256]{0,1:T(8,128)S(1)} %add.123), channel_id=1, source_target_pairs={{0,32},{32,0},{16,48},{48,16},{64,96},{96,64},{80,112},{112,80},{1... | collective-permute-start | bytes 393224 | tf_op jit(solution)/shard_map/ppermute | solution.py:16
  600.7 8.4 %collective-permute-start.6 = (f32[128,256]{0,1:T(8,128)S(1)}, f32[128,256]{0,1:T(8,128)S(1)}, u32[]{:S(2)}, u32[]{:S(2)}) collective-permute-start(f32[128,256]{0,1:T(8,128)S(1)} %add.126), channel_id=1, source_target_pairs={{0,64},{64,0},{16,80},{80,16},{32,96},{96,32},{48,112},{112,48},{1... | collective-permute-start | bytes 393224 | tf_op jit(solution)/shard_map/ppermute | solution.py:16
  609.1 6.9 collective-permute-start.7
  615.9 8.4 %collective-permute-start.8 = (f32[128,256]{0,1:T(8,128)S(1)}, f32[128,256]{0,1:T(8,128)S(1)}, u32[]{:S(2)}, u32[]{:S(2)}) collective-permute-start(f32[128,256]{0,1:T(8,128)S(1)} %add.132), channel_id=1, source_target_pairs={{0,256},{256,0},{16,272},{272,16},{32,288},{288,32},{48,304},{304,... | collective-permute-start | bytes 393224 | tf_op jit(solution)/shard_map/ppermute | solution.py:16
  622.2 5.6 copy-start.10
  622.2 5.8 copy-start.8
  646.7 3.1 copy-start.2
  649.8 2.5 copy-start.4
  658.9 37.6 %copy-start.6 = (f32[128,4096]{0,1:T(8,128)S(1)}, f32[128,4096]{0,1:T(8,128)}, u32[]{:S(2)}) copy-start(f32[128,4096]{0,1:T(8,128)} %copy-done.5) | copy-start | bytes 6291460
  693.7 2.8 copy-start.7
Sparse Core Ops, SparseCore 0:
  625.3 68.3 all-gather.1
where the time goes:
time: 712 us; the launch traced here: 711 us
  waiting for transfers between devices  501 us (70%)
  starting transfers between devices  138 us (19%)
  local copies, waits for them, and re-layouts  26.5 us (4%)
  matrix products  26.3 us (4%)
  between operations  13.8 us (2%)
    ppermute x9, waiting for transfers between devices, swapped(): return lax.ppermute(block, axis, route)  467 us
    ppermute x9, starting transfers between devices, swapped(): return lax.ppermute(block, axis, route)  138 us
    all_gather x1, waiting for transfers between devices, on_device(): lax.all_gather(high_sum, 'sy', axis=1, tiled=True)  34.8 us
    dot_general x4, matrix products, add_level(): jnp.dot(queries_f32, term, precision=lax.Precision.HIGHEST)  14.4 us
  transfers between devices with their start and end apart: 10, of which 10 were waited for; matrix products, arithmetic and copies ran while one was open for 5% of the time, Pallas kernels for 0%

commit v1 on v0

--- a/solution.py
+++ b/solution.py
@@ -4,6 +4,13 @@
 from jax.sharding import PartitionSpec as P
 
 STRETCH = 64
+
+
+def all_by_exchange(x, name, d):
+    size = lax.axis_size(name)
+    parts = jnp.stack([x for _ in range(size)])
+    parts = lax.all_to_all(parts, name, split_axis=0, concat_axis=0)
+    return jnp.concatenate(parts, axis=d)
 
 
 def swapped(block, axis, distance):
@@ -118,9 +125,7 @@
         bits_high,
     )
     outputs = outputs + jnp.dot(
-        queries_f32,
-        lax.all_gather(high_sum, "sy", axis=1, tiled=True),
-        precision=lax.Precision.HIGHEST,
+        queries_f32, all_by_exchange(high_sum, "sy", 1), precision=lax.Precision.HIGHEST
     )
     return outputs.astype(jnp.bfloat16)
 

time: 712 us -> 728 us (1.022)
  the two profiles are of different devices: /device:TPU:4 before, /device:TPU:36 now
where the time goes in v1:
time: 728 us
  waiting for transfers between devices  472 us (65%)
  starting transfers between devices  194 us (27%)
  local copies, waits for them, and re-layouts  28 us (4%)
  matrix products  27.9 us (4%)
    ppermute x9, waiting for transfers between devices, swapped(): return lax.ppermute(block, axis, route)  416 us
    all_to_all x1, starting transfers between devices, all_by_exchange(): parts = lax.all_to_all(parts, name, split_axis=0, concat_axis=0)  149 us
    all_to_all x1, waiting for transfers between devices, all_by_exchange(): parts = lax.all_to_all(parts, name, split_axis=0, concat_axis=0)  56.6 us
    ppermute x9, starting transfers between devices, swapped(): return lax.ppermute(block, axis, route)  45.5 us
    dot_general x4, matrix products, add_level(): jnp.dot(queries_f32, term, precision=lax.Precision.HIGHEST)  16 us
  transfers between devices with their start and end apart: 10, of which 10 were waited for; matrix products, arithmetic and copies ran while one was open for 5% of the time, Pallas kernels for 0%

profile of v1, /device:TPU:36, one launch (start us, length us, event | category | flops | bytes accessed | tf_op | source)
XLA Modules:
  0.0 727.7 jit_solution(7208010800379316985)
XLA Ops:
  2.4 3.0 bitcast_reduce_fusion
  7.5 47.2 %collective-permute-done = f32[128,4096]{0,1:T(8,128)S(1)} collective-permute-done((f32[128,4096]{0,1:T(8,128)S(1)}, f32[128,4096]{0,1:T(8,128)S(1)}, u32[]{:S(2)}, u32[]{:S(2)}) %collective-permute-start) | collective-permute-done | bytes 2097184 | tf_op jit(solution)/shard_map/ppermute | solution.py:23
  56.3 5.2 collective-permute-start.1
  61.5 88.9 %collective-permute-done.1 = f32[128,4096]{0,1:T(8,128)S(1)} collective-permute-done((f32[128,4096]{0,1:T(8,128)S(1)}, f32[128,4096]{0,1:T(8,128)S(1)}, u32[]{:S(2)}, u32[]{:S(2)}) %collective-permute-start.1) | collective-permute-done | bytes 2097184 | tf_op jit(solution)/shard_map/ppermute | solution.py:23
  151.7 9.1 %collective-permute-start.2 = (f32[128,4096]{0,1:T(8,128)S(1)}, f32[128,4096]{0,1:T(8,128)S(1)}, u32[]{:S(2)}, u32[]{:S(2)}) collective-permute-start(f32[128,4096]{0,1:T(8,128)S(1)} %add.113), channel_id=1, source_target_pairs={{0,4},{4,0},{1,5},{5,1},{2,6},{6,2},{3,7},{7,3},{8,12},{12,8},{9,1... | collective-permute-start | bytes 6291464 | tf_op jit(solution)/shard_map/ppermute | solution.py:23
  160.8 133.6 %collective-permute-done.2 = f32[128,4096]{0,1:T(8,128)S(1)} collective-permute-done((f32[128,4096]{0,1:T(8,128)S(1)}, f32[128,4096]{0,1:T(8,128)S(1)}, u32[]{:S(2)}, u32[]{:S(2)}) %collective-permute-start.2) | collective-permute-done | bytes 2097184 | tf_op jit(solution)/shard_map/ppermute | solution.py:23
  296.3 13.2 %collective-permute-start.3 = (f32[128,4096]{0,1:T(8,128)}, f32[128,4096]{0,1:T(8,128)}, u32[]{:S(2)}, u32[]{:S(2)}) collective-permute-start(f32[128,4096]{0,1:T(8,128)} %add.116), channel_id=1, source_target_pairs={{0,8},{8,0},{1,9},{9,1},{2,10},{10,2},{3,11},{11,3},{4,12},{12,4},... | collective-permute-start | bytes 6291464 | tf_op jit(solution)/shard_map/ppermute | solution.py:23
  309.5 129.9 %collective-permute-done.3 = f32[128,4096]{0,1:T(8,128)} collective-permute-done((f32[128,4096]{0,1:T(8,128)}, f32[128,4096]{0,1:T(8,128)}, u32[]{:S(2)}, u32[]{:S(2)}) %collective-permute-start.3) | collective-permute-done | bytes 2097184 | tf_op jit(solution)/shard_map/ppermute | solution.py:23
  443.7 3.1 collective-permute-start.5
  446.8 4.3 collective-permute-done.5
  453.6 5.9 collective-permute-done.6
  459.5 3.5 collective-permute-start.7
  466.4 5.1 collective-permute-start.8
  476.5 148.8 %all-to-all-start = ((f32[16,128,256]{1,2,0:T(8,128)}), f32[16,128,256]{1,2,0:T(8,128)}, u32[]{:S(2)}, u32[]{:S(2)}) async-start(f32[16,128,256]{1,2,0:T(8,128)} %stack.8), calls=%async_computation | async-start | bytes 4194304 | tf_op jit(solution)/shard_map/all_to_all | solution.py:12
  628.2 2.9 convolution_bitcast_fusion.6
  631.1 5.8 copy.19
  637.0 5.4 reshape.219
  642.4 3.0 convolution_bitcast_fusion.5
  646.9 3.0 copy.17
  649.9 2.5 convolution_bitcast_fusion.3
  654.9 4.4 convolution_bitcast_fusion.1
  659.2 56.6 %all-to-all-done = f32[16,128,256]{1,2,0:T(8,128)} async-done(((f32[16,128,256]{1,2,0:T(8,128)}), f32[16,128,256]{1,2,0:T(8,128)}, u32[]{:S(2)}, u32[]{:S(2)}) %all-to-all-start) | async-done | bytes 2097184 | tf_op jit(solution)/shard_map/all_to_all | solution.py:12
  715.8 2.8 convolution_bitcast_fusion
  718.7 6.8 fusion.5
  (75 shorter events, 33.3 us)
Async XLA Ops:
  0.0 2.4 copy-start
  0.0 1.6 copy-start.10
  5.5 49.3 %collective-permute-start = (f32[128,4096]{0,1:T(8,128)S(1)}, f32[128,4096]{0,1:T(8,128)S(1)}, u32[]{:S(2)}, u32[]{:S(2)}) collective-permute-start(f32[128,4096]{0,1:T(8,128)S(1)} %get-tuple-element.16), channel_id=1, source_target_pairs={{0,1},{1,0},{2,3},{3,2},{4,5},{5,4},{6,7},{7,6},{8,9},{9,8},{10,11... | collective-permute-start | bytes 6291464 | tf_op jit(solution)/shard_map/ppermute | solution.py:23
  54.7 1.4 copy-start.5
  56.3 94.1 %collective-permute-start.1 = (f32[128,4096]{0,1:T(8,128)S(1)}, f32[128,4096]{0,1:T(8,128)S(1)}, u32[]{:S(2)}, u32[]{:S(2)}) collective-permute-start(f32[128,4096]{0,1:T(8,128)S(1)} %add.110), channel_id=1, source_target_pairs={{0,2},{2,0},{1,3},{3,1},{4,6},{6,4},{5,7},{7,5},{8,10},{10,8},{9,1... | collective-permute-start | bytes 6291464 | tf_op jit(solution)/shard_map/ppermute | solution.py:23
  150.4 1.3 copy-start.1
  151.7 142.7 %collective-permute-start.2 = (f32[128,4096]{0,1:T(8,128)S(1)}, f32[128,4096]{0,1:T(8,128)S(1)}, u32[]{:S(2)}, u32[]{:S(2)}) collective-permute-start(f32[128,4096]{0,1:T(8,128)S(1)} %add.113), channel_id=1, source_target_pairs={{0,4},{4,0},{1,5},{5,1},{2,6},{6,2},{3,7},{7,3},{8,12},{12,8},{9,1... | collective-permute-start | bytes 6291464 | tf_op jit(solution)/shard_map/ppermute | solution.py:23
  294.4 1.9 copy-start.3
  296.3 143.1 %collective-permute-start.3 = (f32[128,4096]{0,1:T(8,128)}, f32[128,4096]{0,1:T(8,128)}, u32[]{:S(2)}, u32[]{:S(2)}) collective-permute-start(f32[128,4096]{0,1:T(8,128)} %add.116), channel_id=1, source_target_pairs={{0,8},{8,0},{1,9},{9,1},{2,10},{10,2},{3,11},{11,3},{4,12},{12,4},... | collective-permute-start | bytes 6291464 | tf_op jit(solution)/shard_map/ppermute | solution.py:23
  440.4 3.2 collective-permute-start.4
  443.7 7.4 %collective-permute-start.5 = (f32[128,256]{0,1:T(8,128)S(1)}, f32[128,256]{0,1:T(8,128)S(1)}, u32[]{:S(2)}, u32[]{:S(2)}) collective-permute-start(f32[128,256]{0,1:T(8,128)S(1)} %add.123), channel_id=1, source_target_pairs={{0,32},{32,0},{16,48},{48,16},{64,96},{96,64},{80,112},{112,80},{1... | collective-permute-start | bytes 393224 | tf_op jit(solution)/shard_map/ppermute | solution.py:23
  451.1 8.4 %collective-permute-start.6 = (f32[128,256]{0,1:T(8,128)S(1)}, f32[128,256]{0,1:T(8,128)S(1)}, u32[]{:S(2)}, u32[]{:S(2)}) collective-permute-start(f32[128,256]{0,1:T(8,128)S(1)} %add.126), channel_id=1, source_target_pairs={{0,64},{64,0},{16,80},{80,16},{32,96},{96,32},{48,112},{112,48},{1... | collective-permute-start | bytes 393224 | tf_op jit(solution)/shard_map/ppermute | solution.py:23
  459.5 6.9 collective-permute-start.7
  466.4 8.4 %collective-permute-start.8 = (f32[128,256]{0,1:T(8,128)S(1)}, f32[128,256]{0,1:T(8,128)S(1)}, u32[]{:S(2)}, u32[]{:S(2)}) collective-permute-start(f32[128,256]{0,1:T(8,128)S(1)} %add.132), channel_id=1, source_target_pairs={{0,256},{256,0},{16,272},{272,16},{32,288},{288,32},{48,304},{304,... | collective-permute-start | bytes 393224 | tf_op jit(solution)/shard_map/ppermute | solution.py:23
  476.5 239.3 %all-to-all-start = ((f32[16,128,256]{1,2,0:T(8,128)}), f32[16,128,256]{1,2,0:T(8,128)}, u32[]{:S(2)}, u32[]{:S(2)}) async-start(f32[16,128,256]{1,2,0:T(8,128)} %stack.8), calls=%async_computation | async-start | bytes 4194304 | tf_op jit(solution)/shard_map/all_to_all | solution.py:12
  625.3 2.6 copy-start.11
  625.3 2.8 copy-start.9
  646.9 3.0 copy-start.2
  649.9 2.5 copy-start.4
  654.9 63.8 %copy-start.8 = (f32[128,4096]{0,1:T(8,128)S(1)}, f32[128,4096]{0,1:T(8,128)}, u32[]{:S(2)}) copy-start(f32[128,4096]{0,1:T(8,128)} %copy.17) | copy-start | bytes 6291460
  715.8 2.8 copy-start.6
  715.8 2.9 copy-start.7
